TPU v7x, 512 devices: a whole 4x4x16 slice. The times are simulated.
512 devices in a mesh: seq: 128 (over z, x, core), head: 4 (over y).
Axes of the slice: x: 4, y: 4, z: 16, core: 2. Of those that a mesh axis runs over, the one named last changes fastest.
Arguments:
- queries: bfloat16 [32768, 512], P('seq', 'head'), may hold values from -16 to 16
- keys: bfloat16 [32768, 512], P('seq', 'head'), may hold values from -16 to 16
- values: bfloat16 [32768, 512], P('seq', 'head'), may hold values from -16 to 16
- out_weight: bfloat16 [512, 512], replicated, may hold values from -0.5 to 0.5
Outputs:
- mixed: bfloat16 [32768, 512], P(('seq', 'head'))
All inputs are finite; a program needn't handle non-finite values.
Results may differ from a plain program's by a relative error of at most 0.00185.
The roundings to bfloat16 on the way count: a program that leaves them out, or rounds other values in their place, can miss the bound.
Values may be sent and summed in bfloat16 or wider, within the bound.
A program may use at most 128 MiB of HBM per device.

v0:
```python
import math
import jax
import jax.numpy as jnp
from jax import lax
from jax.sharding import PartitionSpec as P

HD = 64
LEAF = 128


def extended_2(cells, sides, width):
    for axis, dim in sides:
        count = lax.axis_size(axis)
        ends = count - 1
        head = lax.slice_in_dim(cells, 0, width, axis=dim)
        tail = lax.slice_in_dim(cells, cells.shape[dim] - width, cells.shape[dim], axis=dim)
        cells = jnp.concatenate(
            [
                lax.ppermute(tail, axis, [(i, (i + 1) % count) for i in range(ends)]),
                cells,
                lax.ppermute(head, axis, [((i + 1) % count, i) for i in range(ends)]),
            ],
            axis=dim,
        )
    return cells


def as_sent(x):

    def short(part):
        return part.astype(jnp.bfloat16) if part.dtype == jnp.float32 else part

    return jax.tree.map(short, x)


def average_pairs(stacked):
    widened = stacked.astype(jnp.float32).reshape(2, stacked.shape[1] // 2, 2, stacked.shape[2])
    return (0.5 * (widened[:, :, 0] + widened[:, :, 1])).astype(jnp.bfloat16)


def near_set(leaf, extended, seq_index, blocks_dev, seq_size):
    positions = jnp.arange(LEAF, dtype=jnp.int32)
    upper_half = positions >= LEAF // 2
    global_leaf = seq_index * blocks_dev + leaf
    all_blocks = seq_size * blocks_dev
    key_parts = [lax.dynamic_slice_in_dim(extended[0], leaf * LEAF, 3 * LEAF, 1)]
    neighbour = global_leaf - 1 + jnp.arange(3 * LEAF, dtype=jnp.int32) // LEAF
    valid_parts = [(neighbour >= 0) & (neighbour < all_blocks)]
    local_block = leaf >> 1
    global_block = global_leaf >> 1
    parity = global_leaf >> 0 & 1
    level_blocks = all_blocks >> 1
    key_parts.append(lax.dynamic_slice_in_dim(extended[1], local_block * LEAF, LEAF, 1))
    key_parts.append(lax.dynamic_slice_in_dim(extended[1], (local_block + 2) * LEAF, LEAF, 1))
    valid_parts.append((global_block >= 1) & jnp.logical_not(upper_half & (parity == 0)))
    valid_parts.append(
        (global_block + 1 < level_blocks)
        & jnp.logical_not(jnp.logical_not(upper_half) & (parity == 1))
    )
    return (jnp.concatenate(key_parts, axis=1), jnp.concatenate(valid_parts, axis=0))


def shards(queries, keys, values, out_weight):
    tok_count = queries.shape[0]
    width = queries.shape[1]
    seq_size = lax.axis_size("seq")
    seq_index = lax.axis_index("seq")
    blocks_dev = tok_count // LEAF
    near_count = blocks_dev.bit_length() - 1
    far_count = max(0, seq_size.bit_length() - 2)
    scale = 1.0 / math.sqrt(HD)
    positions = jnp.arange(LEAF, dtype=jnp.int32)
    upper_half = positions >= LEAF // 2
    local = [jnp.stack([keys, values], axis=0)]
    local.append(average_pairs(local[-1]))
    extended = [extended_2(stacked, (("seq", 1),), LEAF) for stacked in local]
    own_block = local[near_count]
    far_pairs = []
    far_valid = []
    everything = lax.all_gather(own_block, "seq", axis=1, tiled=True)
    for level_far in range(1, far_count + 1):
        everything = average_pairs(everything)
        group = seq_index >> level_far
        padded = jnp.pad(everything, ((0, 0), (LEAF, LEAF), (0, 0)))
        lower = lax.dynamic_slice_in_dim(padded, group * LEAF, LEAF, 1)
        upper = lax.dynamic_slice_in_dim(padded, (group + 2) * LEAF, LEAF, 1)
        far_pairs.append(jnp.concatenate([lower, upper], axis=1))
    for level_far in range(1, far_count + 1):
        group = seq_index >> level_far
        parity = seq_index >> level_far - 1 & 1
        far_valid.append((group >= 1) & jnp.logical_not(upper_half & (parity == 0)))
        far_valid.append(
            (group + 1 < seq_size >> level_far)
            & jnp.logical_not(jnp.logical_not(upper_half) & (parity == 1))
        )
    far_keys = jnp.concatenate(far_pairs, axis=1)
    far_mask = jnp.concatenate(far_valid, axis=0)
    leaves_step = min(blocks_dev, max(1, 512 // LEAF))
    step_count = blocks_dev // leaves_step

    def attend(step):
        leaves = step * leaves_step + jnp.arange(leaves_step, dtype=jnp.int32)
        near_keys, near_mask = jax.vmap(
            lambda leaf: near_set(leaf, extended, seq_index, blocks_dev, seq_size)
        )(leaves)
        query_block = queries.reshape(leaves_step, LEAF, width)
        head_outputs = []
        for head_number in range(width // HD):
            low_col = head_number * HD
            high_col = low_col + HD
            near_scores = (
                jnp.einsum(
                    "nhs,nos->nho",
                    query_block[:, :, low_col:high_col],
                    near_keys[:, 0, :, low_col:high_col],
                    preferred_element_type=jnp.float32,
                )
                * scale
            )
            near_scores = jnp.where(near_mask[:, None, :], near_scores, -jnp.inf)
            peak = jnp.max(near_scores, axis=-1, keepdims=True)
            far_scores = (
                jnp.einsum(
                    "qs,os->qo",
                    queries[:, low_col:high_col],
                    far_keys[0, :, low_col:high_col],
                    preferred_element_type=jnp.float32,
                )
                * scale
            )
            far_scores = far_scores.reshape(leaves_step, LEAF, far_scores.shape[-1])
            far_scores = jnp.where(far_mask[None, None, :], far_scores, -jnp.inf)
            peak = jnp.maximum(peak, jnp.max(far_scores, axis=-1, keepdims=True))
            near_weights = jnp.exp(near_scores - peak)
            total = jnp.sum(near_weights, axis=-1)
            numer = jnp.einsum(
                "fkm,fmp->fkp",
                near_weights.astype(jnp.bfloat16),
                near_keys[:, 1, :, low_col:high_col],
                preferred_element_type=jnp.float32,
            )
            far_weights = jnp.exp(far_scores - peak)
            total = total + jnp.sum(far_weights, axis=-1)
            far_rounded = far_weights.astype(jnp.bfloat16).reshape(
                leaves_step * LEAF, far_weights.shape[-1]
            )
            far_numer = jnp.dot(
                far_rounded, far_keys[1, :, low_col:high_col], preferred_element_type=jnp.float32
            )
            numer = numer + far_numer.reshape(leaves_step, LEAF, HD)
            head_outputs.append((numer / total[..., None]).astype(jnp.bfloat16))
        return jnp.concatenate(head_outputs, axis=-1).reshape(leaves_step * LEAF, width)

    attended = lax.map(attend, jnp.arange(step_count, dtype=jnp.int32)).reshape(tok_count, width)
    gathered_rows = lax.all_to_all(
        as_sent(attended), "head", split_axis=0, concat_axis=1, tiled=True
    ).astype(attended.dtype)
    return jnp.dot(gathered_rows, out_weight, preferred_element_type=jnp.float32).astype(
        jnp.bfloat16
    )


def solution(mesh):
    in_specs = (P("seq", "head"), P("seq", "head"), P("seq", "head"), P())
    out_specs = P(("seq", "head"), None)
    return jax.shard_map(shards, mesh=mesh, in_specs=in_specs, out_specs=out_specs, check_vma=False)
```

profile of v0, /device:TPU:32, one launch (start us, length us, event | category | flops | bytes accessed | tf_op | source)
XLA Modules:
  0.0 354.0 jit_solution(11749175016474953703)
XLA Ops:
  11.6 5.8 %collective-permute-start.3 = (bf16[2,128,128]{2,0,1:T(2,128)(2,1)S(1)}, bf16[2,128,128]{2,0,1:T(2,128)(2,1)S(1)}, u32[]{:S(2)}, u32[]{:S(2)}) collective-permute-start(bf16[2,128,128]{2,0,1:T(2,128)(2,1)S(1)} %fusion.76), channel_id=1, source_target_pairs={{4,0},{8,4},{12,8},{16,12},{20,16},{24,20},{28,24},{32,28},{36,32}... | collective-permute-start | bytes 196616 | tf_op jit(solution)/shard_map/ppermute | solution.py:21
  21.4 5.8 %collective-permute-start.1 = (bf16[2,128,128]{2,0,1:T(2,128)(2,1)S(1)}, bf16[2,128,128]{2,0,1:T(2,128)(2,1)S(1)}, u32[]{:S(2)}, u32[]{:S(2)}) collective-permute-start(bf16[2,128,128]{2,0,1:T(2,128)(2,1)S(1)} %get-tuple-element.46), channel_id=1, source_target_pairs={{4,0},{8,4},{12,8},{16,12},{20,16},{24,20},{28,24},{32,28},{36,32}... | collective-permute-start | bytes 196616 | tf_op jit(solution)/shard_map/ppermute | solution.py:21
  37.7 124.1 %all-gather.3.cloned.1.call-done = bf16[2,16384,1,128]{3,0,2,1:T(2,128)(2,1)} async-done(((bf16[2,128,1,128]{3,0,2,1:T(2,128)(2,1)}), bf16[2,16384,1,128]{3,0,2,1:T(2,128)(2,1)}) %all-gather.3.cloned.1.call-update) | async-done | bytes 8388624 | tf_op jit(solution)/shard_map/all_gather | solution.py:80
  161.8 5.1 %copy.50 = bf16[2,16384,1,128]{3,1,0,2:T(8,128)(2,1)S(1)} copy(bf16[2,16384,1,128]{3,0,2,1:T(2,128)(2,1)} %all-gather.3.cloned.1.call-done) | data formatting | bytes 16777216 | tf_op jit(solution)/shard_map/all_gather | solution.py:80
  166.8 13.0 %fusion.63 = (f32[2,8192,1,128]{3,2,1,0:T(1,128)}, f32[2,8192,1,128]{3,2,1,0:T(1,128)}) fusion(bf16[2,8192,2,128]{3,2,1,0:T(2,128)(2,1)S(1)} %bitcast.97), kind=kLoop, calls=%fused_computation.146 | loop fusion | bytes 33554432 | tf_op jit(solution)/shard_map/slice | solution.py:38
  179.8 18.0 %copy.76 = f32[2,8192,1,128]{1,3,0,2:T(8,128)} copy(f32[2,8192,1,128]{3,2,1,0:T(1,128)} %get-tuple-element.22) | data formatting | bytes 16777216
  197.8 18.0 %copy.77 = f32[2,8192,1,128]{1,3,0,2:T(8,128)} copy(f32[2,8192,1,128]{3,2,1,0:T(1,128)} %get-tuple-element.21) | data formatting | bytes 16777216
  215.8 9.4 %multiply_convert_fusion = bf16[2,8192,1,128]{1,3,0,2:T(8,128)(2,1)} fusion(f32[2,8192,1,128]{1,3,0,2:T(8,128)} %copy.76, f32[2,8192,1,128]{1,3,0,2:T(8,128)} %copy.77), kind=kLoop, calls=%fused_computation.3 | loop fusion | flops 6291456 | bytes 20971520 | tf_op jit(solution)/shard_map/convert_element_type | solution.py:38
  225.2 7.0 %copy.53 = f32[2,8192,1,128]{3,1,0,2:T(8,128)} copy(bf16[2,8192,1,128]{1,3,0,2:T(8,128)(2,1)} %multiply_convert_fusion) | data formatting | bytes 12582912 | tf_op jit(solution)/shard_map/convert_element_type | solution.py:37
  232.3 11.5 %fusion.62 = (f32[2,4096,1,128]{3,2,1,0:T(1,128)}, f32[2,4096,1,128]{3,2,1,0:T(1,128)}) fusion(f32[2,4096,2,128]{3,2,1,0:T(2,128)} %bitcast.102), kind=kLoop, calls=%fused_computation.145 | loop fusion | bytes 16777216 | tf_op jit(solution)/shard_map/slice | solution.py:38
  243.8 10.2 %copy.78 = f32[2,4096,1,128]{1,3,0,2:T(8,128)} copy(f32[2,4096,1,128]{3,2,1,0:T(1,128)} %get-tuple-element.20) | data formatting | bytes 8388608
  254.0 10.2 %copy.79 = f32[2,4096,1,128]{1,3,0,2:T(8,128)} copy(f32[2,4096,1,128]{3,2,1,0:T(1,128)} %get-tuple-element.19) | data formatting | bytes 8388608
  264.1 4.3 %multiply_convert_fusion.1 = bf16[2,4096,1,128]{1,3,0,2:T(8,128)(2,1)S(1)} fusion(f32[2,4096,1,128]{1,3,0,2:T(8,128)} %copy.78, f32[2,4096,1,128]{1,3,0,2:T(8,128)} %copy.79), kind=kLoop, calls=%fused_computation.4 | loop fusion | flops 3145728 | bytes 10485760 | tf_op jit(solution)/shard_map/convert_element_type | solution.py:38
  268.5 2.9 copy.56
  271.4 7.9 %fusion.64 = (f32[2,2048,1,128]{3,2,1,0:T(1,128)}, f32[2,2048,1,128]{3,2,1,0:T(1,128)}) fusion(f32[2,2048,2,128]{3,2,1,0:T(2,128)} %bitcast.105), kind=kLoop, calls=%fused_computation.147 | loop fusion | bytes 8388608 | tf_op jit(solution)/shard_map/slice | solution.py:38
  279.3 6.1 %copy.80 = f32[2,2048,1,128]{1,3,0,2:T(8,128)} copy(f32[2,2048,1,128]{3,2,1,0:T(1,128)} %get-tuple-element.32) | data formatting | bytes 4194304
  285.4 6.1 %copy.81 = f32[2,2048,1,128]{1,3,0,2:T(8,128)} copy(f32[2,2048,1,128]{3,2,1,0:T(1,128)} %get-tuple-element.23) | data formatting | bytes 4194304
  291.5 3.6 %multiply_convert_fusion.2 = bf16[2,2048,1,128]{1,3,0,2:T(8,128)(2,1)} fusion(f32[2,2048,1,128]{1,3,0,2:T(8,128)} %copy.80, f32[2,2048,1,128]{1,3,0,2:T(8,128)} %copy.81), kind=kLoop, calls=%fused_computation.11 | loop fusion | flops 1572864 | bytes 5242880 | tf_op jit(solution)/shard_map/convert_element_type | solution.py:38
  295.1 2.6 copy.59
  297.7 5.4 %fusion.65 = (f32[2,1024,1,128]{3,2,1,0:T(1,128)}, f32[2,1024,1,128]{3,2,1,0:T(1,128)}) fusion(f32[2,1024,2,128]{3,2,1,0:T(2,128)} %bitcast.108), kind=kLoop, calls=%fused_computation.148 | loop fusion | bytes 4194304 | tf_op jit(solution)/shard_map/slice | solution.py:38
  303.1 3.6 %copy.82 = f32[2,1024,1,128]{1,3,0,2:T(8,128)} copy(f32[2,1024,1,128]{3,2,1,0:T(1,128)} %get-tuple-element.36) | data formatting | bytes 2097152
  306.7 3.6 %copy.83 = f32[2,1024,1,128]{1,3,0,2:T(8,128)} copy(f32[2,1024,1,128]{3,2,1,0:T(1,128)} %get-tuple-element.34) | data formatting | bytes 2097152
  313.3 3.5 fusion.66
  336.6 9.7 %all_to_all.19 = bf16[4,64,128]{2,1,0:T(8,128)(2,1)S(1)} all-to-all(bf16[4,64,128]{2,1,0:T(8,128)(2,1)S(1)} %bitcast.121), channel_id=1, replica_groups=mesh['seq'=128,'head'=4] {'head'}, dimensions={0} | all-to-all | bytes 131072 | tf_op jit(solution)/shard_map/all_to_all | solution.py:155
  (125 shorter events, 42.7 us)
Async XLA Ops:
  6.5 339.8 %copy-start = (bf16[512,512]{1,0:T(8,128)(2,1)S(1)}, bf16[512,512]{1,0:T(8,128)(2,1)}, u32[]{:S(2)}) copy-start(bf16[512,512]{1,0:T(8,128)(2,1)} %param.7) | copy-start | bytes 1572868
  6.5 155.2 %all-gather.3.cloned.1.call-start = ((), (), s32[]{:S(2)}) async-start(), calls=%async_computation.1 | async-start | bytes 8454144 | tf_op jit(solution)/shard_map/all_gather | solution.py:80
  9.6 21.1 %collective-permute-start.2 = (bf16[2,128,128]{2,0,1:T(2,128)(2,1)S(1)}, bf16[2,128,128]{2,0,1:T(2,128)(2,1)S(1)}, u32[]{:S(2)}, u32[]{:S(2)}) collective-permute-start(bf16[2,128,128]{2,0,1:T(2,128)(2,1)S(1)} %fusion.76), channel_id=1, source_target_pairs={{0,4},{4,8},{8,12},{12,16},{16,20},{20,24},{24,28},{28,32},{32,36}... | collective-permute-start | bytes 196616 | tf_op jit(solution)/shard_map/ppermute | solution.py:19
  11.6 19.1 %collective-permute-start.3 = (bf16[2,128,128]{2,0,1:T(2,128)(2,1)S(1)}, bf16[2,128,128]{2,0,1:T(2,128)(2,1)S(1)}, u32[]{:S(2)}, u32[]{:S(2)}) collective-permute-start(bf16[2,128,128]{2,0,1:T(2,128)(2,1)S(1)} %fusion.76), channel_id=1, source_target_pairs={{4,0},{8,4},{12,8},{16,12},{20,16},{24,20},{28,24},{32,28},{36,32}... | collective-permute-start | bytes 196616 | tf_op jit(solution)/shard_map/ppermute | solution.py:21
  19.5 13.4 %collective-permute-start = (bf16[2,128,128]{2,0,1:T(2,128)(2,1)S(1)}, bf16[2,128,128]{2,0,1:T(2,128)(2,1)S(1)}, u32[]{:S(2)}, u32[]{:S(2)}) collective-permute-start(bf16[2,128,128]{2,0,1:T(2,128)(2,1)S(1)} %get-tuple-element.45), channel_id=1, source_target_pairs={{0,4},{4,8},{8,12},{12,16},{16,20},{20,24},{24,28},{28,32},{32,36}... | collective-permute-start | bytes 196616 | tf_op jit(solution)/shard_map/ppermute | solution.py:19
  21.4 11.5 %collective-permute-start.1 = (bf16[2,128,128]{2,0,1:T(2,128)(2,1)S(1)}, bf16[2,128,128]{2,0,1:T(2,128)(2,1)S(1)}, u32[]{:S(2)}, u32[]{:S(2)}) collective-permute-start(bf16[2,128,128]{2,0,1:T(2,128)(2,1)S(1)} %get-tuple-element.46), channel_id=1, source_target_pairs={{4,0},{8,4},{12,8},{16,12},{20,16},{24,20},{28,24},{32,28},{36,32}... | collective-permute-start | bytes 196616 | tf_op jit(solution)/shard_map/ppermute | solution.py:21
  32.0 3.3 copy-start.9
  35.2 1.2 copy-start.5
  328.9 2.2 copy-start.1
  331.2 1.2 copy-start.2
  331.3 1.4 copy-start.7
  331.3 1.4 copy-start.8
  332.5 1.1 copy-start.4
  332.6 1.2 copy-start.6
  333.3 1.3 copy-start.3
Sparse Core Ops, SparseCore 0:
  10.5 151.2 all-gather.2
where the time goes:
time: 357 us; the launch traced here: 354 us
  local copies, waits for them, and re-layouts  161 us (45%)
  waiting for transfers between devices  124 us (35%)
  other arithmetic  24 us (7%)
  starting transfers between devices  15.3 us (4%)
  between operations  14 us (4%)
  blocking collectives  9.71 us (3%)
  matrix products  5.36 us (2%)
    all_gather x1, waiting for transfers between devices, shards(): everything = lax.all_gather(own_block, 'seq', axis=1, tiled=True)  124 us
    unnamed x54, local copies, waits for them, and re-layouts  90 us
    slice x6, local copies, waits for them, and re-layouts, average_pairs(): return (0.5 * (widened[:, :, 0] + widened[:, :, 1])).astype(jnp.bfloat16)  43.9 us
    convert_element_type x8, other arithmetic, average_pairs(): return (0.5 * (widened[:, :, 0] + widened[:, :, 1])).astype(jnp.bfloat16)  21.3 us
    convert_element_type x5, local copies, waits for them, and re-layouts, average_pairs(): stacked.astype(jnp.float32)  14.7 us
    ppermute x2, starting transfers between devices, extended_2(): lax.ppermute(head, axis, [((i + 1) % count, i) for i in range(ends)])  11.5 us
    all_to_all x1, blocking collectives, shards(): lax.all_to_all(as_sent(attended), 'head', split_axis=0, concat_axis=1, ti...  9.71 us
  transfers between devices with their start and end apart: 5, of which 1 were waited for; matrix products, arithmetic and copies ran while one was open for 4% of the time, Pallas kernels for 0%

commit v1 on v0

--- a/solution.py
+++ b/solution.py
@@ -77,7 +77,9 @@
     own_block = local[near_count]
     far_pairs = []
     far_valid = []
-    everything = lax.all_gather(own_block, "seq", axis=1, tiled=True)
+    everything = jnp.concatenate(
+        lax.all_to_all(jnp.stack([own_block] * lax.axis_size("seq")), "seq", 0, 0), axis=1
+    )
     for level_far in range(1, far_count + 1):
         everything = average_pairs(everything)
         group = seq_index >> level_far

time: 357 us -> 599 us (1.68)
  the two profiles are of different devices: /device:TPU:32 before, /device:TPU:64 now
where the time goes in v1:
time: 599 us; the launch traced here: 596 us
  waiting for transfers between devices  343 us (57%)
  local copies, waits for them, and re-layouts  167 us (28%)
  other arithmetic  35.5 us (6%)
  starting transfers between devices  34.7 us (6%)
  blocking collectives  9.89 us (2%)
    ppermute x2, waiting for transfers between devices, extended_2(): lax.ppermute(tail, axis, [(i, (i + 1) % count) for i in range(ends)])  343 us
    unnamed x54, local copies, waits for them, and re-layouts  90.1 us
    slice x6, local copies, waits for them, and re-layouts, average_pairs(): return (0.5 * (widened[:, :, 0] + widened[:, :, 1])).astype(jnp.bfloat16)  50.6 us
    convert_element_type x7, other arithmetic, average_pairs(): return (0.5 * (widened[:, :, 0] + widened[:, :, 1])).astype(jnp.bfloat16)  21.5 us
    all_to_all x1, starting transfers between devices, shards(): lax.all_to_all(jnp.stack([own_block] * lax.axis_size('seq')), 'seq', 0, 0)  19.1 us
    convert_element_type x5, local copies, waits for them, and re-layouts, average_pairs(): stacked.astype(jnp.float32)  14.7 us
  transfers between devices with their start and end apart: 5, of which 1 were waited for; matrix products, arithmetic and copies ran while one was open for 2% of the time, Pallas kernels for 0%

profile of v1, /device:TPU:64, one launch (start us, length us, event | category | flops | bytes accessed | tf_op | source)
XLA Modules:
  0.0 596.3 jit_solution(8958414069375583554)
XLA Ops:
  2.4 5.4 stack.20
  7.7 19.1 %all-to-all-start = ((bf16[128,2,128,128]{3,2,1,0:T(8,128)(2,1)}), bf16[128,2,128,128]{3,2,1,0:T(8,128)(2,1)}, u32[]{:S(2)}, u32[]{:S(2)}) async-start(bf16[128,2,128,128]{3,2,1,0:T(8,128)(2,1)} %stack.20), calls=%async_computation | async-start | bytes 16777216 | tf_op jit(solution)/shard_map/all_to_all | solution.py:81
  29.0 5.6 collective-permute-start.3
  37.0 5.9 collective-permute-start.1
  46.5 343.2 %collective-permute-done.2 = bf16[2,128,128]{2,0,1:T(2,128)(2,1)S(1)} collective-permute-done((bf16[2,128,128]{2,0,1:T(2,128)(2,1)S(1)}, bf16[2,128,128]{2,0,1:T(2,128)(2,1)S(1)}, u32[]{:S(2)}, u32[]{:S(2)}) %collective-permute-start.2) | collective-permute-done | bytes 65568 | tf_op jit(solution)/shard_map/ppermute | solution.py:19
  396.7 11.2 %copy_convert_fusion = f32[128,2,128,128]{3,2,0,1:T(8,128)} fusion(bf16[128,2,128,128]{3,2,1,0:T(8,128)(2,1)} %all-to-all-done), kind=kLoop, calls=%fused_computation.3 | loop fusion | flops 4194304 | bytes 25165824 | tf_op jit(solution)/shard_map/convert_element_type | solution.py:37
  407.9 19.3 %fusion.63 = (f32[2,8192,1,128]{3,2,1,0:T(1,128)}, f32[2,8192,1,128]{3,2,1,0:T(1,128)}) fusion(f32[2,8192,2,128]{3,2,1,0:T(2,128)} %bitcast.98), kind=kLoop, calls=%fused_computation.147 | loop fusion | bytes 33554432 | tf_op jit(solution)/shard_map/slice | solution.py:38
  427.2 18.0 %copy.77 = f32[2,8192,1,128]{1,3,0,2:T(8,128)} copy(f32[2,8192,1,128]{3,2,1,0:T(1,128)} %get-tuple-element.20) | data formatting | bytes 16777216
  445.2 18.0 %copy.78 = f32[2,8192,1,128]{1,3,0,2:T(8,128)} copy(f32[2,8192,1,128]{3,2,1,0:T(1,128)} %get-tuple-element.19) | data formatting | bytes 16777216
  463.3 9.4 %multiply_convert_fusion = bf16[2,8192,1,128]{1,3,0,2:T(8,128)(2,1)} fusion(f32[2,8192,1,128]{1,3,0,2:T(8,128)} %copy.77, f32[2,8192,1,128]{1,3,0,2:T(8,128)} %copy.78), kind=kLoop, calls=%fused_computation.4 | loop fusion | flops 6291456 | bytes 20971520 | tf_op jit(solution)/shard_map/convert_element_type | solution.py:38
  472.7 7.0 %copy.54 = f32[2,8192,1,128]{3,1,0,2:T(8,128)} copy(bf16[2,8192,1,128]{1,3,0,2:T(8,128)(2,1)} %multiply_convert_fusion) | data formatting | bytes 12582912 | tf_op jit(solution)/shard_map/convert_element_type | solution.py:37
  479.7 11.8 %fusion.64 = (f32[2,4096,1,128]{3,2,1,0:T(1,128)}, f32[2,4096,1,128]{3,2,1,0:T(1,128)}) fusion(f32[2,4096,2,128]{3,2,1,0:T(2,128)} %bitcast.101), kind=kLoop, calls=%fused_computation.148 | loop fusion | bytes 16777216 | tf_op jit(solution)/shard_map/slice | solution.py:38
  491.5 10.1 %copy.79 = f32[2,4096,1,128]{1,3,0,2:T(8,128)} copy(f32[2,4096,1,128]{3,2,1,0:T(1,128)} %get-tuple-element.22) | data formatting | bytes 8388608
  501.7 10.2 %copy.80 = f32[2,4096,1,128]{1,3,0,2:T(8,128)} copy(f32[2,4096,1,128]{3,2,1,0:T(1,128)} %get-tuple-element.21) | data formatting | bytes 8388608
  511.8 4.3 multiply_convert_fusion.1
  519.1 8.0 %fusion.65 = (f32[2,2048,1,128]{3,2,1,0:T(1,128)}, f32[2,2048,1,128]{3,2,1,0:T(1,128)}) fusion(f32[2,2048,2,128]{3,2,1,0:T(2,128)} %bitcast.104), kind=kLoop, calls=%fused_computation.149 | loop fusion | bytes 8388608 | tf_op jit(solution)/shard_map/slice | solution.py:38
  527.1 6.1 %copy.81 = f32[2,2048,1,128]{1,3,0,2:T(8,128)} copy(f32[2,2048,1,128]{3,2,1,0:T(1,128)} %get-tuple-element.32) | data formatting | bytes 4194304
  533.2 6.1 %copy.82 = f32[2,2048,1,128]{1,3,0,2:T(8,128)} copy(f32[2,2048,1,128]{3,2,1,0:T(1,128)} %get-tuple-element.23) | data formatting | bytes 4194304
  539.3 3.6 multiply_convert_fusion.2
  545.5 5.4 fusion.66
  551.0 3.6 copy.83
  554.6 3.6 copy.84
  561.1 3.5 fusion.67
  585.5 9.9 %all_to_all.24 = bf16[4,64,128]{2,1,0:T(8,128)(2,1)S(1)} all-to-all(bf16[4,64,128]{2,1,0:T(8,128)(2,1)S(1)} %bitcast.120), channel_id=1, replica_groups=mesh['seq'=128,'head'=4] {'head'}, dimensions={0} | all-to-all | bytes 131072 | tf_op jit(solution)/shard_map/all_to_all | solution.py:157
  (125 shorter events, 47.1 us)
Async XLA Ops:
  0.0 595.4 %copy-start = (bf16[512,512]{1,0:T(8,128)(2,1)S(1)}, bf16[512,512]{1,0:T(8,128)(2,1)}, u32[]{:S(2)}) copy-start(bf16[512,512]{1,0:T(8,128)(2,1)} %param.7) | copy-start | bytes 1572868
  7.7 26.8 %copy-start.7 = (bf16[256,128]{1,0:T(8,128)(2,1)S(1)}, bf16[256,128]{1,0:T(8,128)(2,1)}, u32[]{:S(2)}) copy-start(bf16[256,128]{1,0:T(8,128)(2,1)} %param.5) | copy-start | bytes 196612
  7.7 27.0 %copy-start.8 = (bf16[256,128]{1,0:T(8,128)(2,1)S(1)}, bf16[256,128]{1,0:T(8,128)(2,1)}, u32[]{:S(2)}) copy-start(bf16[256,128]{1,0:T(8,128)(2,1)} %param.6) | copy-start | bytes 196612
  7.7 388.9 %all-to-all-start = ((bf16[128,2,128,128]{3,2,1,0:T(8,128)(2,1)}), bf16[128,2,128,128]{3,2,1,0:T(8,128)(2,1)}, u32[]{:S(2)}, u32[]{:S(2)}) async-start(bf16[128,2,128,128]{3,2,1,0:T(8,128)(2,1)} %stack.20), calls=%async_computation | async-start | bytes 16777216 | tf_op jit(solution)/shard_map/all_to_all | solution.py:81
  26.9 362.8 %collective-permute-start.2 = (bf16[2,128,128]{2,0,1:T(2,128)(2,1)S(1)}, bf16[2,128,128]{2,0,1:T(2,128)(2,1)S(1)}, u32[]{:S(2)}, u32[]{:S(2)}) collective-permute-start(bf16[2,128,128]{2,0,1:T(2,128)(2,1)S(1)} %fusion.46), channel_id=1, source_target_pairs={{0,4},{4,8},{8,12},{12,16},{16,20},{20,24},{24,28},{28,32},{32,36}... | collective-permute-start | bytes 196616 | tf_op jit(solution)/shard_map/ppermute | solution.py:19
  29.0 360.7 %collective-permute-start.3 = (bf16[2,128,128]{2,0,1:T(2,128)(2,1)S(1)}, bf16[2,128,128]{2,0,1:T(2,128)(2,1)S(1)}, u32[]{:S(2)}, u32[]{:S(2)}) collective-permute-start(bf16[2,128,128]{2,0,1:T(2,128)(2,1)S(1)} %fusion.46), channel_id=1, source_target_pairs={{4,0},{8,4},{12,8},{16,12},{20,16},{24,20},{28,24},{32,28},{36,32}... | collective-permute-start | bytes 196616 | tf_op jit(solution)/shard_map/ppermute | solution.py:21
  35.1 356.8 %collective-permute-start = (bf16[2,128,128]{2,0,1:T(2,128)(2,1)S(1)}, bf16[2,128,128]{2,0,1:T(2,128)(2,1)S(1)}, u32[]{:S(2)}, u32[]{:S(2)}) collective-permute-start(bf16[2,128,128]{2,0,1:T(2,128)(2,1)S(1)} %get-tuple-element.45), channel_id=1, source_target_pairs={{0,4},{4,8},{8,12},{12,16},{16,20},{20,24},{24,28},{28,32},{32,36}... | collective-permute-start | bytes 196616 | tf_op jit(solution)/shard_map/ppermute | solution.py:19
  37.0 354.8 %collective-permute-start.1 = (bf16[2,128,128]{2,0,1:T(2,128)(2,1)S(1)}, bf16[2,128,128]{2,0,1:T(2,128)(2,1)S(1)}, u32[]{:S(2)}, u32[]{:S(2)}) collective-permute-start(bf16[2,128,128]{2,0,1:T(2,128)(2,1)S(1)} %get-tuple-element.46), channel_id=1, source_target_pairs={{4,0},{8,4},{12,8},{16,12},{20,16},{24,20},{28,24},{32,28},{36,32}... | collective-permute-start | bytes 196616 | tf_op jit(solution)/shard_map/ppermute | solution.py:21
  390.9 3.3 copy-start.9
  394.2 1.2 copy-start.5
  577.9 2.2 copy-start.1
  580.2 1.2 copy-start.2
  581.5 1.1 copy-start.4
  581.5 1.2 copy-start.6
  582.2 1.3 copy-start.3
